TPU v7x, 32 devices: a whole 2x2x4 slice. The times are simulated.
32 devices in a mesh: dp: 4 (over y, x), seq: 8 (over z, core).
Axes of the slice: x: 2, y: 2, z: 4, core: 2. Of those that a mesh axis runs over, the one named last changes fastest.
Arguments:
- trunk_rows: bfloat16 [4, 4096, 1536], P('dp', 'seq'), may hold values from -6 to 6
- head_grad: bfloat16 [4, 4096, 1536], P('dp', None, 'seq'), may hold values from -6 to 6
- decoder_grad: bfloat16 [4, 8192, 768], P('dp', 'seq'), may hold values from -6 to 6
- pair_grad: bfloat16 [4, 256, 256, 128], P('dp', 'seq'), may hold values from -4 to 4
- conv_weight: bfloat16 [5, 1536, 768], P(None, 'dp'), may hold values from -0.09375 to 0.09375
- left_weight: bfloat16 [1536, 128], replicated, may hold values from -0.625 to 0.625
- right_weight: bfloat16 [1536, 128], replicated, may hold values from -0.625 to 0.625
Outputs:
- grad_rows: bfloat16 [4, 4096, 1536], P('dp', 'seq')
- left_weight_grad: float32 [1536, 128], P('seq')
- right_weight_grad: float32 [1536, 128], P('seq')
All inputs are finite; a program needn't handle non-finite values.
Results may differ from a plain program's by a relative error of at most 0.011.
Values may be sent and summed in bfloat16 or wider, within the bound.
A program may use at most 128 MiB of HBM per device.

v0:
```python
import jax
import jax.numpy as jnp
from jax import lax
from jax.sharding import PartitionSpec as P

POOL = 16


def extended(block, sides, width):
    for axis, dim in sides:
        count = lax.axis_size(axis)
        forward = [(i, i + 1) for i in range(count - 1)]
        backward = [(target, source) for source, target in forward]
        low = lax.ppermute(
            lax.slice_in_dim(block, block.shape[dim] - width, None, axis=dim), axis, forward
        )
        high = lax.ppermute(lax.slice_in_dim(block, 0, width, axis=dim), axis, backward)
        block = jnp.concatenate([low, block, high], axis=dim)
    return block


def contract_rows(first_mat, second_mat):
    return lax.dot_general(
        first_mat, second_mat, (((1,), (1,)), ((), ())), preferred_element_type=jnp.float32
    )


def local(trunk_rows, head_grad, decoder_grad, pair_grad, conv_weight, left_weight, right_weight):
    seq_count = lax.axis_size("seq")
    row_count = trunk_rows.shape[1]
    feature_count = trunk_rows.shape[2]
    bin_count = row_count // POOL
    head_local = lax.all_to_all(head_grad, "seq", split_axis=1, concat_axis=2, tiled=True)
    padded = extended(decoder_grad, (("seq", 1),), 2)[0]
    out_count = decoder_grad.shape[1]
    shard_piece = lax.all_gather(conv_weight, "dp", axis=1, tiled=True)
    running = jnp.zeros((out_count, shard_piece.shape[1]), jnp.float32)
    for offset in range(shard_piece.shape[0]):
        running = running + contract_rows(
            padded[4 - offset : 4 - offset + out_count], shard_piece[offset]
        )
    from_decoder = running.reshape(row_count, 2, feature_count).sum(axis=1)
    pooled = (
        trunk_rows[0]
        .astype(jnp.float32)
        .reshape(bin_count, POOL, feature_count)
        .mean(axis=1)
        .astype(jnp.bfloat16)
    )
    left_proj = jnp.dot(pooled, left_weight, preferred_element_type=jnp.float32).astype(
        jnp.bfloat16
    )
    right_all = jnp.dot(
        lax.all_gather(pooled, "seq", axis=0, tiled=True),
        right_weight,
        preferred_element_type=jnp.float32,
    ).astype(jnp.bfloat16)
    pair_block = pair_grad[0]
    left_grad = jnp.einsum(
        "ijc,jc->ic", pair_block, right_all, preferred_element_type=jnp.float32
    ).astype(jnp.bfloat16)
    column_part = jnp.einsum(
        "ijc,ic->jc", pair_block, left_proj, preferred_element_type=jnp.float32
    )
    right_grad = lax.psum_scatter(column_part, "seq", scatter_dimension=0, tiled=True).astype(
        jnp.bfloat16
    )
    pooled_grad = contract_rows(left_grad, left_weight) + contract_rows(right_grad, right_weight)
    from_pair = jnp.repeat(pooled_grad, POOL, axis=0) / POOL
    grad_local = (head_local[0].astype(jnp.float32) + from_decoder + from_pair).astype(jnp.bfloat16)
    left_sum = lax.dot_general(
        pooled, left_grad, (((0,), (0,)), ((), ())), preferred_element_type=jnp.float32
    )
    right_sum = lax.dot_general(
        pooled, right_grad, (((0,), (0,)), ((), ())), preferred_element_type=jnp.float32
    )
    grad_scale = 1.0 / (POOL * lax.axis_size("dp"))
    slice_rows = feature_count // seq_count
    left_total, right_total = lax.psum((left_sum, right_sum), ("dp", "seq"))
    first_index = lax.axis_index("seq") * slice_rows
    left_total = lax.dynamic_slice_in_dim(left_total, first_index, slice_rows, 0)
    right_total = lax.dynamic_slice_in_dim(right_total, first_index, slice_rows, 0)
    return (grad_local[None], left_total * grad_scale, right_total * grad_scale)


def solution(mesh):
    placed = (
        P("dp", "seq", None),
        P("dp", None, "seq"),
        P("dp", "seq", None),
        P("dp", "seq", None, None),
        P(None, "dp", None),
        P(),
        P(),
    )
    return jax.shard_map(
        local,
        mesh=mesh,
        in_specs=placed,
        out_specs=(P("dp", "seq", None), P("seq", None), P("seq", None)),
        check_vma=False,
    )
```

profile of v0, /device:TPU:0, one launch (start us, length us, event | category | flops | bytes accessed | tf_op | source)
XLA Modules:
  0.0 340.3 jit_solution(10442024715826092783)
XLA Ops:
  8.0 0.0 reduce-scatter.4.cloned.1.call-start
  8.1 2.1 convert_reduce_fusion
  10.2 1.2 fusion.16
  11.4 1.1 multiply_reduce_fusion
  12.6 0.0 reduce-scatter.4.cloned.1.call-update
  12.6 0.0 all-reduce.3.cloned.1.call-start
  12.6 17.2 %all_gather.7 = bf16[256,1536]{1,0:T(8,128)(2,1)S(1)} all-gather(bf16[32,1536]{1,0:T(8,128)(2,1)S(1)} %multiply_convert_fusion), channel_id=1, replica_groups=mesh['dp'=4,'seq'=8] {'seq'}, dimensions={0}, use_global_device_ids=true | all-gather | bytes 884736 | tf_op jit(solution)/shard_map/all_gather | solution.py:54
  29.9 0.4 fusion.14
  30.2 0.4 multiply_reduce_fusion.1
  30.7 0.1 copy.30
  30.8 0.6 copy-done.10
  31.4 1.2 fusion.28
  32.6 13.3 %reduce-scatter.4.cloned.1.call-done = f32[32,128]{1,0:T(8,128)} async-done(((f32[256,128]{1,0:T(8,128)}), f32[32,128]{1,0:T(8,128)}) %reduce-scatter.4.cloned.1.call-update) | async-done | bytes 16400
  45.9 0.8 copy.39
  46.8 1.2 fusion.27
  48.0 0.0 all-reduce.3.cloned.1.call-update
  48.0 0.0 all-gather.2.cloned.1.call-start
  48.0 0.5 all-gather.2.cloned.1.call-update
  48.6 8.5 %copy.20 = bf16[1,4096,192]{2,0,1:T(2,128)(2,1)} copy(bf16[1,4096,192]{1,2,0:T(8,128)(2,1)S(1)} %copy-done.6) | data formatting | bytes 3145728 | tf_op args[1]
  57.1 0.5 broadcast.21
  57.6 23.7 %reduce.4 = bf16[4096,192]{1,0:T(8,128)(2,1)S(1)} reduce(bf16[4096,1,192]{2,1,0:T(2,128)(2,1)} %bitcast.82, bf16[]{:T(256)} %broadcast.21), dimensions={1}, to_apply=%bitcast.67.reduce_sub_computation | reduce | bytes 3145730
  81.3 4.4 %reshape.69 = bf16[8,2,49152]{2,1,0:T(2,128)(2,1)} reshape(bf16[4096,192]{1,0:T(8,128)(2,1)S(1)} %reduce.4) | data formatting | bytes 3145728
  85.7 3.7 %all-to-all-start = ((bf16[8,2,49152]{2,1,0:T(2,128)(2,1)}), bf16[8,2,49152]{2,1,0:T(2,128)(2,1)S(1)}, u32[]{:S(2)}, u32[]{:S(2)}) async-start(bf16[8,2,49152]{2,1,0:T(2,128)(2,1)} %reshape.69), calls=%async_computation | async-start | bytes 3145728 | tf_op jit(solution)/shard_map/all_to_all | solution.py:33
  89.4 1.3 collective-permute-start
  90.7 3.2 collective-permute-start.1
  93.9 1.9 fusion.29
  95.9 1.2 constant_dynamic-update-slice_fusion.1
  97.1 0.6 constant_dynamic-update-slice_fusion
  97.7 1.9 fusion.5
  99.6 160.7 %all-reduce.3.cloned.1.call-done = (f32[1536,128]{1,0:T(8,128)}, f32[1536,128]{1,0:T(8,128)}) async-done(((f32[1536,128]{1,0:T(8,128)}, f32[1536,128]{1,0:T(8,128)}), (f32[1536,128]{1,0:T(8,128)}, f32[1536,128]{1,0:T(8,128)})) %all-reduce.3.cloned.1.call-update) | async-done | bytes 1572880 | tf_op jit(solution)/shard_map/psum | solution.py:79
  260.3 1.6 dynamic-slice_multiply_fusion
  261.9 5.0 %reshape.70 = bf16[4096,1,192]{2,1,0:T(2,128)(2,1)} reshape(bf16[8,2,49152]{2,1,0:T(2,128)(2,1)S(1)} %all-to-all-done) | data formatting | bytes 3145728
  266.9 9.9 %copy.21 = bf16[1,4096,192]{1,2,0:T(8,128)(2,1)S(1)} copy(bf16[1,4096,192]{2,0,1:T(2,128)(2,1)} %bitcast.83) | data formatting | bytes 3145728 | tf_op jit(solution)/shard_map/all_to_all | solution.py:33
  276.8 0.3 convert_element_type.71
  277.1 2.7 copy.45
  279.8 1.8 copy.22
  281.7 2.4 copy.23
  284.1 4.9 %fusion.3 = f32[1024,1536]{1,0:T(8,128)S(1)} fusion(bf16[5,1536,768]{2,1,0:T(8,128)(2,1)} %all-gather.2.cloned.1.call-done, bf16[1,1026,768]{2,1,0:T(8,128)(2,1)} %constant_dynamic-update-slice_fusion), kind=kOutput, calls=%fused_computation.13 | convolution fusion | flops 2415919104 | bytes 10223616 | tf_op jit(solution)/shard_map/dot_general | solution.py:23
  289.1 1.1 copy-done.9
  290.1 2.6 fusion.4
  292.8 4.6 %fusion.2 = f32[1024,1536]{1,0:T(8,128)} fusion(bf16[5,1536,768]{2,1,0:T(8,128)(2,1)S(1)} %copy-done.9, bf16[1,1024,768]{2,1,0:T(8,128)(2,1)S(1)} %copy-done.5), kind=kOutput, calls=%fused_computation.11 | convolution fusion | flops 2415919104 | bytes 10223616 | tf_op jit(solution)/shard_map/dot_general | solution.py:23
  297.4 4.7 %fusion.1 = f32[1024,1536]{1,0:T(8,128)} fusion(bf16[5,1536,768]{2,1,0:T(8,128)(2,1)S(1)} %copy-done.9, bf16[1,2,768]{2,1,0:T(2,128)(2,1)S(1)} %collective-permute-done.1, bf16[1,1024,768]{2,1,0:T(8,128)(2,1)S(1)} %copy-done.5), kind=kOutput, calls=%fused_computation.9 | convolution fusion | flops 2419064832 | bytes 10226688 | tf_op jit(solution)/shard_map/dot_general | solution.py:23
  302.1 8.6 %add_add_fusion = f32[1024,1536]{1,0:T(8,128)} fusion(f32[1024,1536]{1,0:T(8,128)} %fusion.1, f32[1024,1536]{1,0:T(8,128)} %fusion.2, f32[1024,1536]{1,0:T(8,128)S(1)} %fusion.4, f32[1024,1536]{1,0:T(8,128)S(1)} %fusion.3, bf16[5,1536,768]{2,1,0:T(8,128)(2,1)} %all-gather.2.cloned.1.call-done, bf16[1,1024,768]{2,1,0:T(8,128)(2,1)S(1)} %copy-done.5, ...), kind=kOutput, calls=%fused_computation | convolution fusion | flops 2425356288 | bytes 35392512 | tf_op jit(solution)/shard_map/dot_general | solution.py:23
  310.6 8.1 %reshape.59 = f32[512,2,1536]{2,1,0:T(2,128)} reshape(f32[1024,1536]{1,0:T(8,128)} %add_add_fusion) | data formatting | bytes 12582912 | tf_op jit(solution)/shard_map/reshape | solution.py:42
  318.8 10.3 %reduce_sum.20 = f32[512,1536]{1,0:T(8,128)S(1)} reduce(f32[512,2,1536]{2,1,0:T(2,128)} %reshape.59, f32[]{:T(128)} %constant.7.clone.1), dimensions={1}, to_apply=%region_0.0 | reduce | flops 786432 | bytes 9437188 | tf_op jit(solution)/shard_map/reduce_sum | solution.py:42
  329.0 0.4 broadcast_in_dim.4
  329.4 1.5 copy-done.2
  330.9 1.9 fusion
  (27 shorter events, 0.1 us)
Async XLA Ops:
  8.0 21.9 %copy-start = (bf16[1536,128]{1,0:T(8,128)(2,1)S(1)}, bf16[1536,128]{1,0:T(8,128)(2,1)}, u32[]{:S(2)}) copy-start(bf16[1536,128]{1,0:T(8,128)(2,1)} %param.13) | copy-start | bytes 1179652
  8.0 3.4 %copy-start.3 = (bf16[1,32,256,128]{3,2,1,0:T(8,128)(2,1)S(1)}, bf16[1,32,256,128]{3,2,1,0:T(8,128)(2,1)}, u32[]{:S(2)}) copy-start(bf16[1,32,256,128]{3,2,1,0:T(8,128)(2,1)} %param.10) | copy-start | bytes 6291460
  8.0 37.9 %reduce-scatter.4.cloned.1.call-start = ((), (), s32[]{:S(2)}) async-start(), calls=%async_computation.3 | async-start | bytes 147456
  12.6 247.7 %all-reduce.3.cloned.1.call-start = ((), (), s32[]{:S(2)}) async-start(), calls=%async_computation.4 | async-start | bytes 3145728 | tf_op jit(solution)/shard_map/psum | solution.py:79
  30.8 0.6 copy-start.10
  32.6 15.9 %copy-start.6 = (bf16[1,4096,192]{1,2,0:T(8,128)(2,1)S(1)}, bf16[1,4096,192]{1,2,0:T(8,128)(2,1)}, u32[]{:S(2)}) copy-start(bf16[1,4096,192]{1,2,0:T(8,128)(2,1)} %param.8) | copy-start | bytes 4718596
  46.7 10.3 %copy-start.11 = (bf16[32,128]{0,1:T(8,128)(2,1)}, bf16[32,128]{0,1:T(8,128)(2,1)S(1)}, u32[]{:S(2)}) copy-start(bf16[32,128]{0,1:T(8,128)(2,1)S(1)} %copy.39) | copy-start | bytes 24580
  48.0 236.1 %all-gather.2.cloned.1.call-start = ((), (), s32[]{:S(2)}) async-start(), calls=%async_computation.2 | async-start | bytes 14745600 | tf_op jit(solution)/shard_map/all_gather | solution.py:36
  85.7 3.7 %copy-start.4 = (bf16[1,1024,768]{2,1,0:T(8,128)(2,1)S(1)}, bf16[1,1024,768]{2,1,0:T(8,128)(2,1)}, u32[]{:S(2)}) copy-start(bf16[1,1024,768]{2,1,0:T(8,128)(2,1)} %param.9) | copy-start | bytes 4718596
  85.7 176.2 %all-to-all-start = ((bf16[8,2,49152]{2,1,0:T(2,128)(2,1)}), bf16[8,2,49152]{2,1,0:T(2,128)(2,1)S(1)}, u32[]{:S(2)}, u32[]{:S(2)}) async-start(bf16[8,2,49152]{2,1,0:T(2,128)(2,1)} %reshape.69), calls=%async_computation | async-start | bytes 3145728 | tf_op jit(solution)/shard_map/all_to_all | solution.py:33
  89.4 7.7 %collective-permute-start = (bf16[1,2,768]{2,1,0:T(2,128)(2,1)S(1)}, bf16[1,2,768]{2,1,0:T(2,128)(2,1)S(1)}, u32[]{:S(2)}, u32[]{:S(2)}) collective-permute-start(bf16[1,2,768]{2,1,0:T(2,128)(2,1)S(1)} %get-tuple-element.11), channel_id=1, source_target_pairs={{1,0},{2,1},{3,2},{4,3},{5,4},{6,5},{7,6},{9,8},{10,9},{11,10},{12... | collective-permute-start | bytes 9224 | tf_op jit(solution)/shard_map/ppermute | solution.py:17
  90.7 206.7 %collective-permute-start.1 = (bf16[1,2,768]{2,1,0:T(2,128)(2,1)S(1)}, bf16[1,2,768]{2,1,0:T(2,128)(2,1)S(1)}, u32[]{:S(2)}, u32[]{:S(2)}) collective-permute-start(bf16[1,2,768]{2,1,0:T(2,128)(2,1)S(1)} %get-tuple-element.12), channel_id=1, source_target_pairs={{0,1},{1,2},{2,3},{3,4},{4,5},{5,6},{6,7},{8,9},{9,10},{10,11},{11... | collective-permute-start | bytes 9224 | tf_op jit(solution)/shard_map/ppermute | solution.py:14
  284.1 4.9 %copy-start.7 = (bf16[1,1026,768]{2,1,0:T(8,128)(2,1)S(1)}, bf16[1,1026,768]{2,1,0:T(8,128)(2,1)}, u32[]{:S(2)}) copy-start(bf16[1,1026,768]{2,1,0:T(8,128)(2,1)} %constant_dynamic-update-slice_fusion) | copy-start | bytes 4727812
  284.1 6.0 %copy-start.9 = (bf16[5,1536,768]{2,1,0:T(8,128)(2,1)S(1)}, bf16[5,1536,768]{2,1,0:T(8,128)(2,1)}, u32[]{:S(2)}) copy-start(bf16[5,1536,768]{2,1,0:T(8,128)(2,1)} %all-gather.2.cloned.1.call-done) | copy-start | bytes 35389444
  290.1 2.6 copy-start.5
  318.8 10.3 %copy-start.8 = (f32[32,1536]{1,0:T(8,128)S(1)}, f32[32,1536]{1,0:T(8,128)}, u32[]{:S(2)}) copy-start(f32[32,1536]{1,0:T(8,128)} %fusion.5) | copy-start | bytes 589828
  329.0 1.9 copy-start.2
  329.4 3.4 %copy-start.1 = (bf16[1536,128]{1,0:T(8,128)(2,1)S(1)}, bf16[1536,128]{1,0:T(8,128)(2,1)}, u32[]{:S(2)}) copy-start(bf16[1536,128]{1,0:T(8,128)(2,1)} %param.13) | copy-start | bytes 1179652
Sparse Core Ops, SparseCore 0:
  12.7 33.1 reduce-scatter.3
  52.3 207.9 all-reduce.2
Sparse Core Ops, SparseCore 1:
  50.3 115.0 all-gather.1
where the time goes:
time: 341 us; the launch traced here: 340 us
  waiting for transfers between devices  175 us (51%)
  local copies, waits for them, and re-layouts  49.8 us (15%)
  other arithmetic  41.6 us (12%)
  matrix products  33.2 us (10%)
  blocking collectives  17.2 us (5%)
  between operations  15.7 us (5%)
  starting transfers between devices  8.34 us (2%)
    psum x1, waiting for transfers between devices, local(): left_total, right_total = lax.psum((left_sum, right_sum), ('dp', 'seq'))  161 us
    dot_general x7, matrix products, contract_rows(): lax.dot_general(first_mat, second_mat, (((1,), (1,)), ((), ())), preferre...  29.2 us
    unnamed x31, local copies, waits for them, and re-layouts  26.4 us
    unnamed x3, other arithmetic  25.3 us
    all_gather x1, blocking collectives, local(): lax.all_gather(pooled, 'seq', axis=0, tiled=True)  17.2 us
    unnamed x4, waiting for transfers between devices  13.8 us
    reduce_sum x1, other arithmetic, local(): from_decoder = running.reshape(row_count, 2, feature_count).sum(axis=1)  10.3 us
    all_to_all x1, local copies, waits for them, and re-layouts, local(): lax.all_to_all(head_grad, 'seq', split_axis=1, concat_axis=2, tiled=True)  9.89 us
  transfers between devices with their start and end apart: 6, of which 2 were waited for; matrix products, arithmetic and copies ran while one was open for 24% of the time, Pallas kernels for 0%

commit v1 on v0

v1 whole, which is shorter than its diff:
```python
import functools

import jax
import jax.numpy as jnp
from jax import lax
from jax.experimental import pallas as pl
from jax.experimental.pallas import tpu as pltpu
from jax.sharding import PartitionSpec as P

POOL = 16
MESH = pl.DeviceIdType.MESH
F32 = jnp.float32
BF16 = jnp.bfloat16


def dot_nt(a, b):
    return lax.dot_general(a, b, (((1,), (1,)), ((), ())), preferred_element_type=F32)


def dot_tn(a, b):
    return lax.dot_general(a, b, (((0,), (0,)), ((), ())), preferred_element_type=F32)


def kernel(
    n, ns,
    trunk_hbm, head_hbm, dec_hbm, pair_hbm, conv_hbm, lw_hbm, rw_hbm,
    out_ref, lwg_ref, rwg_ref,
    trunk, lw, rw, pair, dec, wbuf, xbuf, decf, halo,
    hl, hs, hc, hr, acc,
    pooled, pslot, precv, rp_own, rp_all, rpf, lpf, col, crecv, lgf, g_own, g_all, parts, pg,
    loc_sem, hl_sem, hs_send, hs_recv, hr_send, hr_recv, halo_send, halo_recv,
    ex_send, ex_recv, wi_send, wi_recv, ws_send, ws_recv, d_send, d_recv,
):
    d = lax.axis_index("dp")
    me = lax.axis_index("seq")
    nz = ns // 2
    z = me // 2
    c = me % 2
    sib = me + 1 - 2 * c
    rows, feats = trunk.shape
    bins = pooled.shape[0]
    width = head_hbm.shape[1]
    taps, shard, emb = conv_hbm.shape
    half = shard // 2
    ecut = emb // 2
    drows = dec.shape[0]
    chunks = emb // 128

    def remote(src, dst, ssem, rsem, dp, seq):
        return pltpu.make_async_remote_copy(
            src_ref=src, dst_ref=dst, send_sem=ssem, recv_sem=rsem,
            device_id=(dp, seq), device_id_type=MESH,
        )

    barrier = pltpu.get_barrier_semaphore()
    for o in range(1, ns):
        pl.semaphore_signal(barrier, inc=1, device_id=(d, lax.rem(me + o, ns)), device_id_type=MESH)
    for o in range(1, n):
        pl.semaphore_signal(barrier, inc=1, device_id=(lax.rem(d + o, n), me), device_id_type=MESH)

    locals_ = [
        pltpu.make_async_copy(src, dst, loc_sem.at[i])
        for i, (src, dst) in enumerate(
            [(trunk_hbm, trunk), (lw_hbm, lw), (rw_hbm, rw), (pair_hbm, pair), (dec_hbm, dec),
             (conv_hbm, wbuf.at[d])]
        )
    ]
    for copy in locals_:
        copy.start()
    head_local = [
        pltpu.make_async_copy(
            head_hbm.at[pl.ds(pl.multiple_of((2 * t + c) * rows, 16), rows)], hl.at[t], hl_sem.at[t]
        )
        for t in range(nz)
    ]
    for copy in head_local:
        copy.start()
    pl.semaphore_wait(barrier, ns - 1 + n - 1)

    def piece(q):
        return (pl.ds(0, taps), pl.ds(pl.multiple_of(c * half, 16), half), pl.ds(q * ecut, ecut))

    def piece_other(q):
        return (pl.ds(0, taps), pl.ds(pl.multiple_of((1 - c) * half, 16), half), pl.ds(q * ecut, ecut))

    def w_copy(from_hbm, owner, q, dp, slot):
        dst = wbuf.at[(owner,) + piece(q)]
        src = conv_hbm.at[piece(q)] if from_hbm else dst
        return remote(src, dst, wi_send.at[slot], wi_recv.at[owner, q], dp, me)

    def w_wait(owner, q):
        w_copy(False, owner, q, lax.rem(d + 1, n), 0).wait_recv()

    def s_copy(owner, q):
        ref = wbuf.at[(owner,) + piece(q)]
        return remote(ref, ref, ws_send.at[owner, q], ws_recv.at[owner, q], d, sib)

    def s_wait(owner, q):
        ref = wbuf.at[(owner,) + piece_other(q)]
        remote(ref, ref, ws_send.at[owner, q], ws_recv.at[owner, q], d, sib).wait_recv()

    sends = []

    def go(copy):
        copy.start()
        sends.append(copy)

    if n == 4:
        xn = d + 1 - 2 * lax.rem(d, 2)
        yn = lax.rem(d + 2, 4)
        dg = 3 - d
        go(w_copy(True, d, 0, xn, 0))
        go(w_copy(True, d, 1, yn, 1))
        go(w_copy(True, d, 1, xn, 2))
        go(w_copy(True, d, 0, yn, 3))
    else:
        for o in range(1, n):
            for q in range(2):
                go(w_copy(True, d, q, lax.rem(d + o, n), 2 * (o - 1) + q))

    for t in range(nz):
        go(remote(
            head_hbm.at[pl.ds(pl.multiple_of((2 * t + 1 - c) * rows, 16), rows)], hs.at[t],
            hs_send.at[t], hs_recv.at[t], d, sib,
        ))

    up = remote(dec_hbm.at[pl.ds(drows - 16, 16)], halo.at[0], halo_send.at[0], halo_recv.at[0],
                d, lax.rem(me + 1, ns))
    down = remote(dec_hbm.at[pl.ds(0, 16)], halo.at[1], halo_send.at[1], halo_recv.at[1],
                  d, lax.rem(me + ns - 1, ns))
    up.start()
    down.start()

    def exchange(kind, src_of, dst):
        for o in range(1, ns):
            t = lax.rem(me + o, ns)
            go(remote(src_of(t), dst.at[me], ex_send.at[kind, o], ex_recv.at[kind, me], d, t))

    def exchange_wait(kind, dst):
        for o in range(1, ns):
            t = lax.rem(me + o, ns)
            remote(dst.at[t], dst.at[t], ex_send.at[kind, o], ex_recv.at[kind, t], d, t).wait_recv()

    locals_[0].wait()
    locals_[1].wait()
    locals_[2].wait()
    row = lax.broadcasted_iota(jnp.int32, (bins, rows), 1)
    first = lax.broadcasted_iota(jnp.int32, (bins, rows), 0) * POOL
    pool_mat = jnp.where((row >= first) & (row < first + POOL), 1.0 / POOL, 0.0).astype(BF16)
    pooled[...] = jnp.dot(pool_mat, trunk[...], preferred_element_type=F32).astype(BF16)
    right = jnp.dot(pooled[...], rw[...], preferred_element_type=F32).astype(BF16)
    rp_own[...] = right
    rp_all[me] = right
    exchange(0, lambda t: rp_own, rp_all)
    lpf[...] = jnp.dot(pooled[...], lw[...], preferred_element_type=F32).astype(BF16).astype(F32)
    for s in range(ns):
        pslot[s] = pooled[:, s * width:(s + 1) * width]
    precv[me] = pslot[me]

    locals_[3].wait()
    bin_all = pair.shape[1]
    for j in range(bin_all // 128):
        def add_row(i, total):
            return total + pair[i, j * 128:(j + 1) * 128, :].astype(F32) * lpf[pl.ds(i, 1), :]
        total = lax.fori_loop(0, bins, add_row, jnp.zeros((128, 128), F32), unroll=4)
        per = 128 // bins
        for s in range(per):
            col[j * per + s] = total[s * bins:(s + 1) * bins]
    exchange(1, lambda t: col.at[t], crecv)
    crecv[me] = col[me]
    exchange(2, lambda t: pslot.at[t], precv)

    def merge(t, dst, dst_index):
        @pl.when(c == 0)
        def _():
            dst[dst_index] = jnp.concatenate([hl[t], hs[t]], axis=1)

        @pl.when(c == 1)
        def _():
            dst[dst_index] = jnp.concatenate([hs[t], hl[t]], axis=1)

    for t in range(nz):
        head_local[t].wait()
        remote(hs.at[t], hs.at[t], hs_send.at[t], hs_recv.at[t], d, sib).wait_recv()
    for o in range(1, nz):
        t = lax.rem(z + o, nz)
        merge(t, hc, t)
        go(remote(hc.at[t], hr.at[z], hr_send.at[o], hr_recv.at[z], d, 2 * t + c))
    merge(z, hr, z)

    exchange_wait(0, rp_all)
    rpf[...] = rp_all[...].reshape(bin_all, 128).astype(F32)

    def row_sum(i, _):
        lgf[pl.ds(i, 1), :] = jnp.sum(pair[i].astype(F32) * rpf[...], axis=0, keepdims=True)
        return 0

    lax.fori_loop(0, bins, row_sum, 0, unroll=2)
    left_grad = lgf[...].astype(BF16)
    exchange_wait(1, crecv)
    right_sum = crecv[0]
    for s in range(1, ns):
        right_sum = right_sum + crecv[s]
    right_grad = right_sum.astype(BF16)
    g_own[:, 0:128] = left_grad
    g_own[:, 128:256] = right_grad
    g_all[me] = g_own[...]
    exchange(3, lambda t: g_own, g_all)

    locals_[4].wait()
    up.wait()
    down.wait()
    for k in range(chunks):
        lanes = slice(k * 128, (k + 1) * 128)
        decf[k, 0:8] = jnp.where(me > 0, halo[0, 8:16, lanes].astype(F32), 0.0)
        decf[k, 8 + drows:16 + drows] = jnp.where(me < ns - 1, halo[1, 0:8, lanes].astype(F32), 0.0)

        @pl.loop(0, drows // 256)
        def _(b):
            decf[k, pl.ds(pl.multiple_of(8 + b * 256, 8), 256)] = dec[
                pl.ds(pl.multiple_of(b * 256, 256), 256), lanes
            ].astype(F32)

        @pl.loop(0, rows // 128)
        def _(b):
            lines = [decf[k, pl.ds(b * 256 + 8 + o, 128, stride=2), :] for o in range(-2, 4)]
            for tap in range(taps):
                pick = 2 - tap + 2
                xbuf[tap, pl.ds(pl.multiple_of(b * 128, 128), 128), lanes] = (
                    lines[pick] + lines[pick + 1]
                ).astype(BF16)

    def conv(owner):
        @pl.loop(0, rows // 256)
        def _(b):
            block = pl.ds(pl.multiple_of(b * 256, 256), 256)
            total = dot_nt(xbuf[0, block, :], wbuf[owner, 0])
            for tap in range(1, taps):
                total = total + dot_nt(xbuf[tap, block, :], wbuf[owner, tap])
            acc[owner, block, :] = total

    def finish_pair():
        exchange_wait(3, g_all)
        exchange_wait(2, precv)
        part = dot_tn(precv[0], g_all[0])
        for s in range(1, ns):
            part = part + dot_tn(precv[s], g_all[s])
        parts[d] = part.astype(BF16)
        for o in range(1, n):
            go(remote(parts.at[d], parts.at[d], d_send.at[o], d_recv.at[d], lax.rem(d + o, n), me))
        pg[...] = (
            dot_nt(g_own[:, 0:128], lw[...]) + dot_nt(g_own[:, 128:256], rw[...])
        ) * (1.0 / POOL)

    locals_[5].wait()
    if n == 4:
        w_wait(xn, 0)
        go(w_copy(False, xn, 0, yn, 4))
        w_wait(yn, 1)
        go(w_copy(False, yn, 1, xn, 5))
        go(s_copy(xn, 0))
        go(s_copy(yn, 1))
        conv(d)
        finish_pair()
        w_wait(xn, 1)
        go(s_copy(xn, 1))
        w_wait(yn, 0)
        go(s_copy(yn, 0))
        for owner in (xn, yn):
            for q in range(2):
                s_wait(owner, q)
            conv(owner)
        for q in range(2):
            w_wait(dg, q)
            go(s_copy(dg, q))
        for q in range(2):
            s_wait(dg, q)
        conv(dg)
    else:
        conv(d)
        finish_pair()

        def others(o, _):
            owner = lax.rem(d + o, n)
            for q in range(2):
                w_wait(owner, q)
                s_copy(owner, q).start()
            for q in range(2):
                s_wait(owner, q)
            conv(owner)
            for q in range(2):
                s_copy(owner, q).wait_send()
            return 0

        lax.fori_loop(1, n, others, 0)

    for o in range(1, n):
        t = lax.rem(d + o, n)
        remote(parts.at[t], parts.at[t], d_send.at[o], d_recv.at[t], t, me).wait_recv()
    total = parts[0].astype(F32)
    for t in range(1, n):
        total = total + parts[t].astype(F32)
    total = total * (1.0 / (POOL * n))
    lwg_ref[...] = total[:, 0:128]
    rwg_ref[...] = total[:, 128:256]

    for o in range(1, nz):
        t = lax.rem(z + o, nz)
        remote(hr.at[t], hr.at[t], hr_send.at[o], hr_recv.at[t], d, 2 * t + c).wait_recv()

    @pl.loop(0, bins)
    def _(b):
        block = pl.ds(pl.multiple_of(b * POOL, POOL), POOL)
        head = jnp.concatenate([hr[t, block, :].astype(F32) for t in range(nz)], axis=1)
        conv_part = jnp.concatenate([acc[t, block, :] for t in range(n)], axis=1)
        out_ref[block, :] = (head + conv_part + pg[pl.ds(b, 1), :]).astype(BF16)

    for copy in sends:
        copy.wait_send()


def local(n, ns, trunk_rows, head_grad, decoder_grad, pair_grad, conv_weight, left_weight, right_weight):
    rows, feats = trunk_rows.shape[1:]
    width = head_grad.shape[2]
    drows, emb = decoder_grad.shape[1:]
    bins, bin_all, chan = pair_grad.shape[1:]
    taps, shard = conv_weight.shape[:2]
    nz = ns // 2
    dma = pltpu.SemaphoreType.DMA
    out, left, right = pl.pallas_call(
        functools.partial(kernel, n, ns),
        out_shape=(
            jax.ShapeDtypeStruct((rows, feats), BF16),
            jax.ShapeDtypeStruct((width, chan), F32),
            jax.ShapeDtypeStruct((width, chan), F32),
        ),
        in_specs=[pl.BlockSpec(memory_space=pl.ANY)] * 7,
        out_specs=(pl.BlockSpec(memory_space=pltpu.VMEM),) * 3,
        scratch_shapes=[
            pltpu.VMEM((rows, feats), BF16),
            pltpu.VMEM((feats, chan), BF16),
            pltpu.VMEM((feats, chan), BF16),
            pltpu.VMEM((bins, bin_all, chan), BF16),
            pltpu.VMEM((drows, emb), BF16),
            pltpu.VMEM((n, taps, shard, emb), BF16),
            pltpu.VMEM((taps, rows, emb), BF16),
            pltpu.VMEM((emb // 128, drows + 16, 128), F32),
            pltpu.VMEM((2, 16, emb), BF16),
            pltpu.VMEM((nz, rows, width), BF16),
            pltpu.VMEM((nz, rows, width), BF16),
            pltpu.VMEM((nz, rows, 2 * width), BF16),
            pltpu.VMEM((nz, rows, 2 * width), BF16),
            pltpu.VMEM((n, rows, shard), F32),
            pltpu.VMEM((bins, feats), BF16),
            pltpu.VMEM((ns, bins, width), BF16),
            pltpu.VMEM((ns, bins, width), BF16),
            pltpu.VMEM((bins, chan), BF16),
            pltpu.VMEM((ns, bins, chan), BF16),
            pltpu.VMEM((bin_all, chan), F32),
            pltpu.VMEM((bins, chan), F32),
            pltpu.VMEM((ns, bins, chan), F32),
            pltpu.VMEM((ns, bins, chan), F32),
            pltpu.VMEM((bins, chan), F32),
            pltpu.VMEM((bins, 2 * chan), BF16),
            pltpu.VMEM((ns, bins, 2 * chan), BF16),
            pltpu.VMEM((n, width, 2 * chan), BF16),
            pltpu.VMEM((bins, feats), F32),
            dma((6,)), dma((nz,)), dma((nz,)), dma((nz,)), dma((nz,)), dma((nz,)), dma((2,)), dma((2,)),
            dma((4, ns)), dma((4, ns)), dma((2 * n,)), dma((n, 2)), dma((n, 2)), dma((n, 2)),
            dma((n,)), dma((n,)),
        ],
        compiler_params=pltpu.CompilerParams(
            collective_id=0, has_side_effects=True, vmem_limit_bytes=56 * 1024 * 1024
        ),
    )(
        trunk_rows[0], head_grad[0], decoder_grad[0], pair_grad[0], conv_weight, left_weight, right_weight
    )
    return out[None], left, right


def solution(mesh):
    placed = (
        P("dp", "seq", None),
        P("dp", None, "seq"),
        P("dp", "seq", None),
        P("dp", "seq", None, None),
        P(None, "dp", None),
        P(),
        P(),
    )
    return jax.shard_map(
        functools.partial(local, mesh.shape["dp"], mesh.shape["seq"]),
        mesh=mesh,
        in_specs=placed,
        out_specs=(P("dp", "seq", None), P("seq", None), P("seq", None)),
        check_vma=False,
    )
```

time: 341 us -> 76.6 us (0.22)
  waiting for transfers between devices: 175 us -> 0 us
  Pallas kernels: 0 us -> 67.9 us
  local copies, waits for them, and re-layouts: 49.8 us -> 7.84 us
  other arithmetic: 41.6 us -> 0 us
  matrix products: 33.2 us -> 0 us
  blocking collectives: 17.2 us -> 0 us
  between operations: 15.7 us -> 0.66 us
  starting transfers between devices: 8.34 us -> 0 us
    psum x1 -> x0, waiting for transfers between devices: 161 us -> none  [local(): left_total, right_total = lax.psum((left_sum, right_sum), ('dp', 'seq'))]
    pallas_call x0 -> x1, Pallas kernels: none -> 67.9 us  [local(): pl.pallas_call(functools.partial(kernel, n, ns), out_shape=(jax.ShapeDtyp...]
    dot_general x11 -> x0, matrix products: 33.2 us -> none  [the longest x7 29.2 us: contract_rows(): lax.dot_general(first_mat, second_mat, (((1,), (1,)), ((), ())), preferre...]
    unnamed x3 -> x0, other arithmetic: 25.3 us -> none
    unnamed x31 -> x8, local copies, waits for them, and re-layouts: 26.4 us -> 7.84 us
    all_gather x1 -> x0, blocking collectives: 17.2 us -> none  [local(): lax.all_gather(pooled, 'seq', axis=0, tiled=True)]
    unnamed x4 -> x0, waiting for transfers between devices: 13.8 us -> none
    reduce_sum x2 -> x0, other arithmetic: 12.4 us -> none  [the longest x1 10.3 us: local(): from_decoder = running.reshape(row_count, 2, feature_count).sum(axis=1)]
  transfers between devices with their start and end apart: 6 -> 0, of which waited for: 2 -> 0; matrix products, arithmetic and copies ran while one was open for 24% -> 0% of each run, Pallas kernels for 0% -> 0%
where the time goes in v1:
time: 76.6 us; the launch traced here: 76.4 us
  Pallas kernels  67.9 us (89%)
  local copies, waits for them, and re-layouts  7.84 us (10%)
    pallas_call x1, Pallas kernels, local(): pl.pallas_call(functools.partial(kernel, n, ns), out_shape=(jax.ShapeDtyp...  67.9 us
    unnamed x8, local copies, waits for them, and re-layouts  7.84 us

profile of v1, /device:TPU:0, one launch (start us, length us, event | category | flops | bytes accessed | tf_op | source)
XLA Modules:
  0.0 76.4 jit_solution(4208253438436222317)
XLA Ops:
  0.6 3.9 %copy.10 = bf16[1,4096,192]{2,1,0:T(8,128)(2,1)} copy(bf16[1,4096,192]{1,2,0:T(8,128)(2,1)} %param.8) | data formatting | bytes 3145728 | tf_op args[1]
  4.5 67.9 %shard_map.94 = (bf16[512,1536]{1,0:T(8,128)(2,1)}, f32[192,128]{1,0:T(8,128)}, f32[192,128]{1,0:T(8,128)}) custom-call(bf16[512,1536]{1,0:T(8,128)(2,1)} %bitcast.8, bf16[4096,192]{1,0:T(8,128)(2,1)} %bitcast.5, bf16[1024,768]{1,0:T(8,128)(2,1)} %bitcast.9, bf16[32,256,128]{2,1,0:T(8,128)(2,1)} %bitcast.6, bf16[5,384,768]{2,1,0:T(8,128)(2,1)} %conv_hbm.1, ...), custom_call_target="tpu_custom_call" | custom-call | tf_op jit(solution)/shard_map/pallas_call | solution.py:330
  72.4 0.0 copy-start.1
  72.4 0.0 copy-start
  72.4 2.7 %copy.14 = bf16[1,512,1536]{2,1,0:T(8,128)(2,1)} copy(bf16[1,512,1536]{2,1,0:T(8,128)(2,1)} %bitcast.7) | data formatting | bytes 3145728
  75.1 0.0 copy-done.1
  75.1 0.6 copy.15
  75.7 0.0 copy-done
  75.7 0.6 copy.16
Async XLA Ops:
  72.4 2.7 %copy-start.1 = (f32[192,128]{1,0:T(8,128)S(1)}, f32[192,128]{1,0:T(8,128)}, u32[]{:S(2)}) copy-start(f32[192,128]{1,0:T(8,128)} %get-tuple-element.13) | copy-start | bytes 294916
  72.4 3.3 %copy-start = (f32[192,128]{1,0:T(8,128)S(1)}, f32[192,128]{1,0:T(8,128)}, u32[]{:S(2)}) copy-start(f32[192,128]{1,0:T(8,128)} %get-tuple-element.14) | copy-start | bytes 294916

commit v2 on v1

--- a/solution.py
+++ b/solution.py
@@ -24,22 +24,20 @@
 def kernel(
     n, ns,
     trunk_hbm, head_hbm, dec_hbm, pair_hbm, conv_hbm, lw_hbm, rw_hbm,
-    out_ref, lwg_ref, rwg_ref,
+    out_ref, both_ref,
     trunk, lw, rw, pair, dec, wbuf, xbuf, decf, halo,
-    hl, hs, hc, hr, acc,
-    pooled, pslot, precv, rp_own, rp_all, rpf, lpf, col, crecv, lgf, g_own, g_all, parts, pg,
-    loc_sem, hl_sem, hs_send, hs_recv, hr_send, hr_recv, halo_send, halo_recv,
+    hr, acc,
+    pooled, pslot, precv, rp_own, rp_all, rpf, lpf, col, crecv, lgf, g_own, g_all, gx, parts,
+    loc_sem, hr_send, hr_recv, halo_send, halo_recv,
     ex_send, ex_recv, wi_send, wi_recv, ws_send, ws_recv, d_send, d_recv,
 ):
     d = lax.axis_index("dp")
     me = lax.axis_index("seq")
-    nz = ns // 2
-    z = me // 2
     c = me % 2
     sib = me + 1 - 2 * c
     rows, feats = trunk.shape
     bins = pooled.shape[0]
-    width = head_hbm.shape[1]
+    width = head_hbm.shape[0]
     taps, shard, emb = conv_hbm.shape
     half = shard // 2
     ecut = emb // 2
@@ -58,22 +56,20 @@
     for o in range(1, n):
         pl.semaphore_signal(barrier, inc=1, device_id=(lax.rem(d + o, n), me), device_id_type=MESH)
 
+    def head_part(t):
+        return head_hbm.at[:, pl.ds(pl.multiple_of(t * rows, 128), rows)]
+
+    def feature_rows(t):
+        return pl.ds(pl.multiple_of(t * width, 16), width)
+
     locals_ = [
         pltpu.make_async_copy(src, dst, loc_sem.at[i])
         for i, (src, dst) in enumerate(
             [(trunk_hbm, trunk), (lw_hbm, lw), (rw_hbm, rw), (pair_hbm, pair), (dec_hbm, dec),
-             (conv_hbm, wbuf.at[d])]
+             (conv_hbm, wbuf.at[d]), (head_part(me), hr.at[feature_rows(me)])]
         )
     ]
     for copy in locals_:
-        copy.start()
-    head_local = [
-        pltpu.make_async_copy(
-            head_hbm.at[pl.ds(pl.multiple_of((2 * t + c) * rows, 16), rows)], hl.at[t], hl_sem.at[t]
-        )
-        for t in range(nz)
-    ]
-    for copy in head_local:
         copy.start()
     pl.semaphore_wait(barrier, ns - 1 + n - 1)
 
@@ -118,11 +114,13 @@
             for q in range(2):
                 go(w_copy(True, d, q, lax.rem(d + o, n), 2 * (o - 1) + q))
 
-    for t in range(nz):
-        go(remote(
-            head_hbm.at[pl.ds(pl.multiple_of((2 * t + 1 - c) * rows, 16), rows)], hs.at[t],
-            hs_send.at[t], hs_recv.at[t], d, sib,
-        ))
+    def head_copy(o, t, owner):
+        return remote(
+            head_part(t), hr.at[feature_rows(owner)], hr_send.at[o], hr_recv.at[owner], d, t
+        )
+
+    for o in range(1, ns):
+        go(head_copy(o, lax.rem(me + o, ns), me))
 
     up = remote(dec_hbm.at[pl.ds(drows - 16, 16)], halo.at[0], halo_send.at[0], halo_recv.at[0],
                 d, lax.rem(me + 1, ns))
@@ -170,43 +168,6 @@
     crecv[me] = col[me]
     exchange(2, lambda t: pslot.at[t], precv)
 
-    def merge(t, dst, dst_index):
-        @pl.when(c == 0)
-        def _():
-            dst[dst_index] = jnp.concatenate([hl[t], hs[t]], axis=1)
-
-        @pl.when(c == 1)
-        def _():
-            dst[dst_index] = jnp.concatenate([hs[t], hl[t]], axis=1)
-
-    for t in range(nz):
-        head_local[t].wait()
-        remote(hs.at[t], hs.at[t], hs_send.at[t], hs_recv.at[t], d, sib).wait_recv()
-    for o in range(1, nz):
-        t = lax.rem(z + o, nz)
-        merge(t, hc, t)
-        go(remote(hc.at[t], hr.at[z], hr_send.at[o], hr_recv.at[z], d, 2 * t + c))
-    merge(z, hr, z)
-
-    exchange_wait(0, rp_all)
-    rpf[...] = rp_all[...].reshape(bin_all, 128).astype(F32)
-
-    def row_sum(i, _):
-        lgf[pl.ds(i, 1), :] = jnp.sum(pair[i].astype(F32) * rpf[...], axis=0, keepdims=True)
-        return 0
-
-    lax.fori_loop(0, bins, row_sum, 0, unroll=2)
-    left_grad = lgf[...].astype(BF16)
-    exchange_wait(1, crecv)
-    right_sum = crecv[0]
-    for s in range(1, ns):
-        right_sum = right_sum + crecv[s]
-    right_grad = right_sum.astype(BF16)
-    g_own[:, 0:128] = left_grad
-    g_own[:, 128:256] = right_grad
-    g_all[me] = g_own[...]
-    exchange(3, lambda t: g_own, g_all)
-
     locals_[4].wait()
     up.wait()
     down.wait()
@@ -230,14 +191,46 @@
                     lines[pick] + lines[pick + 1]
                 ).astype(BF16)
 
+    def row_sums():
+        exchange_wait(0, rp_all)
+        rpf[...] = rp_all[...].reshape(bin_all, 128).astype(F32)
+
+        def row_sum(i, _):
+            lgf[pl.ds(i, 1), :] = jnp.sum(pair[i].astype(F32) * rpf[...], axis=0, keepdims=True)
+            return 0
+
+        lax.fori_loop(0, bins, row_sum, 0, unroll=2)
+        left_grad = lgf[...].astype(BF16)
+        exchange_wait(1, crecv)
+        right_sum = crecv[0]
+        for s in range(1, ns):
+            right_sum = right_sum + crecv[s]
+        right_grad = right_sum.astype(BF16)
+        g_own[:, 0:128] = left_grad
+        g_own[:, 128:256] = right_grad
+        gx[...] = dot_tn(pool_mat, g_own[...]).astype(BF16)
+        g_all[me] = g_own[...]
+        exchange(3, lambda t: g_own, g_all)
+
+    unit = (
+        lax.broadcasted_iota(jnp.int32, (256, 256), 0) == lax.broadcasted_iota(jnp.int32, (256, 256), 1)
+    ).astype(BF16)
+
     def conv(owner):
+        feature = pl.ds(pl.multiple_of(owner * shard, 16), shard)
+
         @pl.loop(0, rows // 256)
         def _(b):
             block = pl.ds(pl.multiple_of(b * 256, 256), 256)
-            total = dot_nt(xbuf[0, block, :], wbuf[owner, 0])
-            for tap in range(1, taps):
+            total = dot_nt(unit, hr[feature, block])
+            total = total + dot_nt(gx[block, 0:128], lw[feature, :])
+            total = total + dot_nt(gx[block, 128:256], rw[feature, :])
+            for tap in range(taps):
                 total = total + dot_nt(xbuf[tap, block, :], wbuf[owner, tap])
-            acc[owner, block, :] = total
+            if shard % 128 == 0:
+                out_ref[block, pl.ds(pl.multiple_of(owner * shard, 128), shard)] = total.astype(BF16)
+            else:
+                acc[owner, block, :] = total.astype(BF16)
 
     def finish_pair():
         exchange_wait(3, g_all)
@@ -248,24 +241,29 @@
         parts[d] = part.astype(BF16)
         for o in range(1, n):
             go(remote(parts.at[d], parts.at[d], d_send.at[o], d_recv.at[d], lax.rem(d + o, n), me))
-        pg[...] = (
-            dot_nt(g_own[:, 0:128], lw[...]) + dot_nt(g_own[:, 128:256], rw[...])
-        ) * (1.0 / POOL)
-
-    locals_[5].wait()
+
+    def finish_head():
+        locals_[5].wait()
+        locals_[6].wait()
+        for o in range(1, ns):
+            t = lax.rem(me + o, ns)
+            head_copy(o, t, t).wait_recv()
+
     if n == 4:
         w_wait(xn, 0)
         go(w_copy(False, xn, 0, yn, 4))
+        go(s_copy(xn, 0))
         w_wait(yn, 1)
         go(w_copy(False, yn, 1, xn, 5))
-        go(s_copy(xn, 0))
         go(s_copy(yn, 1))
-        conv(d)
-        finish_pair()
+        row_sums()
         w_wait(xn, 1)
         go(s_copy(xn, 1))
         w_wait(yn, 0)
         go(s_copy(yn, 0))
+        finish_pair()
+        finish_head()
+        conv(d)
         for owner in (xn, yn):
             for q in range(2):
                 s_wait(owner, q)
@@ -277,8 +275,10 @@
             s_wait(dg, q)
         conv(dg)
     else:
+        row_sums()
+        finish_pair()
+        finish_head()
         conv(d)
-        finish_pair()
 
         def others(o, _):
             owner = lax.rem(d + o, n)
@@ -300,20 +300,15 @@
     total = parts[0].astype(F32)
     for t in range(1, n):
         total = total + parts[t].astype(F32)
-    total = total * (1.0 / (POOL * n))
-    lwg_ref[...] = total[:, 0:128]
-    rwg_ref[...] = total[:, 128:256]
-
-    for o in range(1, nz):
-        t = lax.rem(z + o, nz)
-        remote(hr.at[t], hr.at[t], hr_send.at[o], hr_recv.at[t], d, 2 * t + c).wait_recv()
-
-    @pl.loop(0, bins)
-    def _(b):
-        block = pl.ds(pl.multiple_of(b * POOL, POOL), POOL)
-        head = jnp.concatenate([hr[t, block, :].astype(F32) for t in range(nz)], axis=1)
-        conv_part = jnp.concatenate([acc[t, block, :] for t in range(n)], axis=1)
-        out_ref[block, :] = (head + conv_part + pg[pl.ds(b, 1), :]).astype(BF16)
+    both_ref[...] = total * (1.0 / (POOL * n))
+
+    if shard % 128 != 0:
+        @pl.loop(0, bins)
+        def _(b):
+            block = pl.ds(pl.multiple_of(b * POOL, POOL), POOL)
+            out_ref[block, :] = jnp.concatenate(
+                [acc[t, block, :].astype(F32) for t in range(n)], axis=1
+            ).astype(BF16)
 
     for copy in sends:
         copy.wait_send()
@@ -325,17 +320,16 @@
     drows, emb = decoder_grad.shape[1:]
     bins, bin_all, chan = pair_grad.shape[1:]
     taps, shard = conv_weight.shape[:2]
-    nz = ns // 2
+    spare = (n, rows, shard) if shard % 128 != 0 else (1, 16, 128)
     dma = pltpu.SemaphoreType.DMA
-    out, left, right = pl.pallas_call(
+    out, both = pl.pallas_call(
         functools.partial(kernel, n, ns),
         out_shape=(
             jax.ShapeDtypeStruct((rows, feats), BF16),
-            jax.ShapeDtypeStruct((width, chan), F32),
-            jax.ShapeDtypeStruct((width, chan), F32),
+            jax.ShapeDtypeStruct((width, 2 * chan), F32),
         ),
         in_specs=[pl.BlockSpec(memory_space=pl.ANY)] * 7,
-        out_specs=(pl.BlockSpec(memory_space=pltpu.VMEM),) * 3,
+        out_specs=(pl.BlockSpec(memory_space=pltpu.VMEM),) * 2,
         scratch_shapes=[
             pltpu.VMEM((rows, feats), BF16),
             pltpu.VMEM((feats, chan), BF16),
@@ -346,11 +340,8 @@
             pltpu.VMEM((taps, rows, emb), BF16),
             pltpu.VMEM((emb // 128, drows + 16, 128), F32),
             pltpu.VMEM((2, 16, emb), BF16),
-            pltpu.VMEM((nz, rows, width), BF16),
-            pltpu.VMEM((nz, rows, width), BF16),
-            pltpu.VMEM((nz, rows, 2 * width), BF16),
-            pltpu.VMEM((nz, rows, 2 * width), BF16),
-            pltpu.VMEM((n, rows, shard), F32),
+            pltpu.VMEM((feats, rows), BF16),
+            pltpu.VMEM(spare, BF16),
             pltpu.VMEM((bins, feats), BF16),
             pltpu.VMEM((ns, bins, width), BF16),
             pltpu.VMEM((ns, bins, width), BF16),
@@ -363,9 +354,9 @@
             pltpu.VMEM((bins, chan), F32),
             pltpu.VMEM((bins, 2 * chan), BF16),
             pltpu.VMEM((ns, bins, 2 * chan), BF16),
+            pltpu.VMEM((rows, 2 * chan), BF16),
             pltpu.VMEM((n, width, 2 * chan), BF16),
-            pltpu.VMEM((bins, feats), F32),
-            dma((6,)), dma((nz,)), dma((nz,)), dma((nz,)), dma((nz,)), dma((nz,)), dma((2,)), dma((2,)),
+            dma((7,)), dma((ns,)), dma((ns,)), dma((2,)), dma((2,)),
             dma((4, ns)), dma((4, ns)), dma((2 * n,)), dma((n, 2)), dma((n, 2)), dma((n, 2)),
             dma((n,)), dma((n,)),
         ],
@@ -373,9 +364,9 @@
             collective_id=0, has_side_effects=True, vmem_limit_bytes=56 * 1024 * 1024
         ),
     )(
-        trunk_rows[0], head_grad[0], decoder_grad[0], pair_grad[0], conv_weight, left_weight, right_weight
+        trunk_rows[0], jnp.swapaxes(head_grad[0], 0, 1), decoder_grad[0], pair_grad[0], conv_weight, left_weight, right_weight
     )
-    return out[None], left, right
+    return out[None], both[:, :chan], both[:, chan:]
 
 
 def solution(mesh):

time: 76.6 us -> 73.5 us (0.960)
  local copies, waits for them, and re-layouts: 7.84 us -> 4.28 us
    unnamed x8 -> x1, local copies, waits for them, and re-layouts: 7.84 us -> 2.65 us
    slice x0 -> x1, local copies, waits for them, and re-layouts: none -> 1.63 us  [local(): return (out[None], both[:, :chan], both[:, chan:])]
where the time goes in v2:
time: 73.5 us; the launch traced here: 73.4 us
  Pallas kernels  68.4 us (93%)
  local copies, waits for them, and re-layouts  4.28 us (6%)
    pallas_call x1, Pallas kernels, local(): pl.pallas_call(functools.partial(kernel, n, ns), out_shape=(jax.ShapeDtyp...  68.4 us
    unnamed x1, local copies, waits for them, and re-layouts  2.65 us
    slice x1, local copies, waits for them, and re-layouts, local(): return (out[None], both[:, :chan], both[:, chan:])  1.63 us

profile of v2, /device:TPU:0, one launch (start us, length us, event | category | flops | bytes accessed | tf_op | source)
XLA Modules:
  0.0 73.4 jit_solution(13375124372635827180)
XLA Ops:
  0.6 68.4 %shard_map.94 = (bf16[512,1536]{1,0:T(8,128)(2,1)}, f32[192,256]{1,0:T(8,128)}) custom-call(bf16[512,1536]{1,0:T(8,128)(2,1)} %bitcast.8, bf16[192,4096]{1,0:T(8,128)(2,1)} %bitcast.9, bf16[1024,768]{1,0:T(8,128)(2,1)} %bitcast.10, bf16[32,256,128]{2,1,0:T(8,128)(2,1)} %bitcast.7, bf16[5,384,768]{2,1,0:T(8,128)(2,1)} %conv_hbm.1, bf16[1536,128]{1,0:T(8,128)(2,1)} %lw_hbm.1, ...), custom_call_target="tpu_custom_call" | custom-call | tf_op jit(solution)/shard_map/pallas_call | solution.py:325
  69.1 1.6 %fusion = (f32[192,128]{1,0:T(8,128)}, f32[192,128]{1,0:T(8,128)}) fusion(f32[192,256]{1,0:T(8,128)} %get-tuple-element.6), kind=kLoop, calls=%fused_computation | loop fusion | bytes 393216 | tf_op jit(solution)/shard_map/slice | solution.py:369
  70.7 2.7 %copy.11 = bf16[1,512,1536]{2,1,0:T(8,128)(2,1)} copy(bf16[1,512,1536]{2,1,0:T(8,128)(2,1)} %bitcast.11) | data formatting | bytes 3145728

commit v3 on v2

--- a/solution.py
+++ b/solution.py
@@ -119,7 +119,7 @@
             head_part(t), hr.at[feature_rows(owner)], hr_send.at[o], hr_recv.at[owner], d, t
         )
 
-    for o in range(1, ns):
+    for o in sorted(range(1, ns), key=lambda o: abs(2 * o - ns)):
         go(head_copy(o, lax.rem(me + o, ns), me))
 
     up = remote(dec_hbm.at[pl.ds(drows - 16, 16)], halo.at[0], halo_send.at[0], halo_recv.at[0],
@@ -217,20 +217,27 @@
     ).astype(BF16)
 
     def conv(owner):
+        @pl.loop(0, rows // 256)
+        def _(b):
+            block = pl.ds(pl.multiple_of(b * 256, 256), 256)
+            total = dot_nt(xbuf[0, block, :], wbuf[owner, 0])
+            for tap in range(1, taps):
+                total = total + dot_nt(xbuf[tap, block, :], wbuf[owner, tap])
+            acc[owner, block, :] = total
+
+    def finish(owner):
         feature = pl.ds(pl.multiple_of(owner * shard, 16), shard)
 
         @pl.loop(0, rows // 256)
         def _(b):
             block = pl.ds(pl.multiple_of(b * 256, 256), 256)
-            total = dot_nt(unit, hr[feature, block])
+            total = acc[owner, block, :] + dot_nt(unit, hr[feature, block])
             total = total + dot_nt(gx[block, 0:128], lw[feature, :])
             total = total + dot_nt(gx[block, 128:256], rw[feature, :])
-            for tap in range(taps):
-                total = total + dot_nt(xbuf[tap, block, :], wbuf[owner, tap])
             if shard % 128 == 0:
                 out_ref[block, pl.ds(pl.multiple_of(owner * shard, 128), shard)] = total.astype(BF16)
             else:
-                acc[owner, block, :] = total.astype(BF16)
+                acc[owner, block, :] = total
 
     def finish_pair():
         exchange_wait(3, g_all)
@@ -243,7 +250,6 @@
             go(remote(parts.at[d], parts.at[d], d_send.at[o], d_recv.at[d], lax.rem(d + o, n), me))
 
     def finish_head():
-        locals_[5].wait()
         locals_[6].wait()
         for o in range(1, ns):
             t = lax.rem(me + o, ns)
@@ -257,13 +263,13 @@
         go(w_copy(False, yn, 1, xn, 5))
         go(s_copy(yn, 1))
         row_sums()
+        locals_[5].wait()
+        conv(d)
         w_wait(xn, 1)
         go(s_copy(xn, 1))
         w_wait(yn, 0)
         go(s_copy(yn, 0))
         finish_pair()
-        finish_head()
-        conv(d)
         for owner in (xn, yn):
             for q in range(2):
                 s_wait(owner, q)
@@ -277,7 +283,7 @@
     else:
         row_sums()
         finish_pair()
-        finish_head()
+        locals_[5].wait()
         conv(d)
 
         def others(o, _):
@@ -302,12 +308,18 @@
         total = total + parts[t].astype(F32)
     both_ref[...] = total * (1.0 / (POOL * n))
 
+    finish_head()
+
+    @pl.loop(0, n)
+    def _(owner):
+        finish(owner)
+
     if shard % 128 != 0:
         @pl.loop(0, bins)
         def _(b):
             block = pl.ds(pl.multiple_of(b * POOL, POOL), POOL)
             out_ref[block, :] = jnp.concatenate(
-                [acc[t, block, :].astype(F32) for t in range(n)], axis=1
+                [acc[t, block, :] for t in range(n)], axis=1
             ).astype(BF16)
 
     for copy in sends:
@@ -320,7 +332,6 @@
     drows, emb = decoder_grad.shape[1:]
     bins, bin_all, chan = pair_grad.shape[1:]
     taps, shard = conv_weight.shape[:2]
-    spare = (n, rows, shard) if shard % 128 != 0 else (1, 16, 128)
     dma = pltpu.SemaphoreType.DMA
     out, both = pl.pallas_call(
         functools.partial(kernel, n, ns),
@@ -341,7 +352,7 @@
             pltpu.VMEM((emb // 128, drows + 16, 128), F32),
             pltpu.VMEM((2, 16, emb), BF16),
             pltpu.VMEM((feats, rows), BF16),
-            pltpu.VMEM(spare, BF16),
+            pltpu.VMEM((n, rows, shard), F32),
             pltpu.VMEM((bins, feats), BF16),
             pltpu.VMEM((ns, bins, width), BF16),
             pltpu.VMEM((ns, bins, width), BF16),

time: 73.5 us -> 72.8 us (level)
  Pallas kernels: 68.4 us -> 67.6 us
    pallas_call x1, Pallas kernels: 68.4 us -> 67.6 us  [local(): pl.pallas_call(functools.partial(kernel, n, ns), out_shape=(jax.ShapeDtyp...]
where the time goes in v3:
time: 72.8 us; the launch traced here: 72.5 us
  Pallas kernels  67.6 us (93%)
  local copies, waits for them, and re-layouts  4.28 us (6%)
    pallas_call x1, Pallas kernels, local(): pl.pallas_call(functools.partial(kernel, n, ns), out_shape=(jax.ShapeDtyp...  67.6 us
    unnamed x1, local copies, waits for them, and re-layouts  2.65 us
    slice x1, local copies, waits for them, and re-layouts, local(): return (out[None], both[:, :chan], both[:, chan:])  1.63 us

profile of v3, /device:TPU:0, one launch (start us, length us, event | category | flops | bytes accessed | tf_op | source)
XLA Modules:
  0.0 72.5 jit_solution(18193299338741437779)
XLA Ops:
  0.6 67.6 %shard_map.94 = (bf16[512,1536]{1,0:T(8,128)(2,1)}, f32[192,256]{1,0:T(8,128)}) custom-call(bf16[512,1536]{1,0:T(8,128)(2,1)} %bitcast.8, bf16[192,4096]{1,0:T(8,128)(2,1)} %bitcast.9, bf16[1024,768]{1,0:T(8,128)(2,1)} %bitcast.10, bf16[32,256,128]{2,1,0:T(8,128)(2,1)} %bitcast.7, bf16[5,384,768]{2,1,0:T(8,128)(2,1)} %conv_hbm.1, bf16[1536,128]{1,0:T(8,128)(2,1)} %lw_hbm.1, ...), custom_call_target="tpu_custom_call" | custom-call | tf_op jit(solution)/shard_map/pallas_call | solution.py:336
  68.3 1.6 %fusion = (f32[192,128]{1,0:T(8,128)}, f32[192,128]{1,0:T(8,128)}) fusion(f32[192,256]{1,0:T(8,128)} %get-tuple-element.6), kind=kLoop, calls=%fused_computation | loop fusion | bytes 393216 | tf_op jit(solution)/shard_map/slice | solution.py:380
  69.9 2.7 %copy.11 = bf16[1,512,1536]{2,1,0:T(8,128)(2,1)} copy(bf16[1,512,1536]{2,1,0:T(8,128)(2,1)} %bitcast.11) | data formatting | bytes 3145728

commit v4 on v3

--- a/solution.py
+++ b/solution.py
@@ -114,20 +114,20 @@
             for q in range(2):
                 go(w_copy(True, d, q, lax.rem(d + o, n), 2 * (o - 1) + q))
 
-    def head_copy(o, t, owner):
-        return remote(
-            head_part(t), hr.at[feature_rows(owner)], hr_send.at[o], hr_recv.at[owner], d, t
-        )
-
-    for o in sorted(range(1, ns), key=lambda o: abs(2 * o - ns)):
-        go(head_copy(o, lax.rem(me + o, ns), me))
-
     up = remote(dec_hbm.at[pl.ds(drows - 16, 16)], halo.at[0], halo_send.at[0], halo_recv.at[0],
                 d, lax.rem(me + 1, ns))
     down = remote(dec_hbm.at[pl.ds(0, 16)], halo.at[1], halo_send.at[1], halo_recv.at[1],
                   d, lax.rem(me + ns - 1, ns))
     up.start()
     down.start()
+
+    def head_copy(o, t, owner):
+        return remote(
+            head_part(t), hr.at[feature_rows(owner)], hr_send.at[o], hr_recv.at[owner], d, t
+        )
+
+    for o in sorted(range(1, ns), key=lambda o: abs(2 * o - ns)):
+        go(head_copy(o, lax.rem(me + o, ns), me))
 
     def exchange(kind, src_of, dst):
         for o in range(1, ns):

time: 72.8 us -> 72.7 us (level)
  no operation moved by 1% of the time
where the time goes in v4:
time: 72.7 us; the launch traced here: 72.5 us
  Pallas kernels  67.6 us (93%)
  local copies, waits for them, and re-layouts  4.28 us (6%)
    pallas_call x1, Pallas kernels, local(): pl.pallas_call(functools.partial(kernel, n, ns), out_shape=(jax.ShapeDtyp...  67.6 us
    unnamed x1, local copies, waits for them, and re-layouts  2.65 us
    slice x1, local copies, waits for them, and re-layouts, local(): return (out[None], both[:, :chan], both[:, chan:])  1.63 us

profile of v4, /device:TPU:0, one launch (start us, length us, event | category | flops | bytes accessed | tf_op | source)
XLA Modules:
  0.0 72.5 jit_solution(6323453804065743000)
XLA Ops:
  0.6 67.6 %shard_map.94 = (bf16[512,1536]{1,0:T(8,128)(2,1)}, f32[192,256]{1,0:T(8,128)}) custom-call(bf16[512,1536]{1,0:T(8,128)(2,1)} %bitcast.8, bf16[192,4096]{1,0:T(8,128)(2,1)} %bitcast.9, bf16[1024,768]{1,0:T(8,128)(2,1)} %bitcast.10, bf16[32,256,128]{2,1,0:T(8,128)(2,1)} %bitcast.7, bf16[5,384,768]{2,1,0:T(8,128)(2,1)} %conv_hbm.1, bf16[1536,128]{1,0:T(8,128)(2,1)} %lw_hbm.1, ...), custom_call_target="tpu_custom_call" | custom-call | tf_op jit(solution)/shard_map/pallas_call | solution.py:336
  68.2 1.6 %fusion = (f32[192,128]{1,0:T(8,128)}, f32[192,128]{1,0:T(8,128)}) fusion(f32[192,256]{1,0:T(8,128)} %get-tuple-element.6), kind=kLoop, calls=%fused_computation | loop fusion | bytes 393216 | tf_op jit(solution)/shard_map/slice | solution.py:380
  69.8 2.7 %copy.11 = bf16[1,512,1536]{2,1,0:T(8,128)(2,1)} copy(bf16[1,512,1536]{2,1,0:T(8,128)(2,1)} %bitcast.11) | data formatting | bytes 3145728
